TPU v7x, 512 devices: a whole 4x8x8 slice. The times are simulated.
512 devices in a mesh: dp: 256 (over x, z, y), cent: 2 (over core).
Axes of the slice: x: 4, y: 8, z: 8, core: 2. Of those that a mesh axis runs over, the one named last changes fastest.
Arguments:
- tokens: float32 [30720, 128], P('dp'), may hold values from -6 to 6
- centroids: float32 [32768, 128], P(('dp', 'cent')), may hold values from -6 to 6
Outputs:
- new_centroids: float32 [32768, 128], P(('dp', 'cent'))
- residuals: float32 [30720, 128], P('dp')
All inputs are finite; a program needn't handle non-finite values.
Results may differ from a plain program's by a relative error of at most 0.0005.
The roundings to bfloat16 on the way count: a program that leaves them out, or rounds other values in their place, can miss the bound.
Values may be sent and summed in bfloat16 or wider, within the bound.
A program may use at most 64 MiB of HBM per device.

v0:
```python
import jax
import jax.numpy as jnp
from jax import lax
from jax.sharding import PartitionSpec as P

ITERS = 3
KB = 2048
EPSILON = 1e-06
SOFTMAX_WARMTH = 0.05


def normalized_rows(values):
    return values * lax.rsqrt(jnp.mean(values * values, axis=-1, keepdims=True) + EPSILON)


def exponent_block(token_half_rows, block):
    affinity_scores = lax.dot_general(
        token_half_rows, block, (((1,), (1,)), ((), ())), preferred_element_type=jnp.float32
    )
    return jnp.exp((affinity_scores / token_half_rows.shape[1] - 1.0) / SOFTMAX_WARMTH)


def shards(tokens, centroids):
    rows_here, feature_dim = tokens.shape
    unit_tok = normalized_rows(tokens)
    token_half_rows = unit_tok.astype(jnp.bfloat16)
    own_rows = normalized_rows(centroids).astype(jnp.bfloat16)
    columns = lax.all_gather(own_rows, "dp", axis=0, tiled=True)
    col_count = columns.shape[0]
    block_count = col_count // KB
    blocks = columns.reshape(block_count, KB, feature_dim)
    col_mass = rows_here * lax.axis_size("dp") / (col_count * lax.axis_size("cent"))
    scales = jnp.ones((block_count, KB), jnp.float32)
    assignment_weight = jnp.ones((rows_here,), jnp.float32)
    for step_index in range(ITERS):

        def row_step(total, packed):
            kernel = exponent_block(token_half_rows, packed[0])
            return (total + jnp.sum(kernel * packed[1][None, :], axis=1), None)

        row_half = lax.scan(row_step, jnp.zeros((rows_here,), jnp.float32), (blocks, scales))[0]
        row_sum = lax.psum(row_half, "cent")
        assignment_weight = 1.0 / row_sum

        def col_only(block):
            kernel = exponent_block(token_half_rows, block)
            return jnp.sum(kernel * assignment_weight[:, None], axis=0)

        col_flat = lax.map(col_only, blocks).reshape(col_count)
        col_total = lax.psum(col_flat, "dp")
        scales = (col_mass / col_total).reshape(block_count, KB)
    weights_bf = assignment_weight.astype(jnp.bfloat16)
    pieces = (
        lax.all_gather(token_half_rows, "dp", axis=0, tiled=True),
        lax.all_gather(weights_bf, "dp", axis=0, tiled=True),
    )
    kernel = exponent_block(pieces[0], own_rows)
    assign_bf = (kernel * pieces[1].astype(jnp.float32)[:, None]).astype(jnp.bfloat16)
    sums_own = lax.dot_general(
        assign_bf, pieces[0], (((0,), (0,)), ((), ())), preferred_element_type=jnp.float32
    )
    new_own = normalized_rows(sums_own)
    fresh = lax.all_gather(new_own.astype(jnp.bfloat16), "dp", axis=0, tiled=True)
    fresh_blocks = fresh.reshape(block_count, KB, feature_dim)

    def soft_step(total, packed):
        kernel = exponent_block(token_half_rows, packed[0])
        transport_plan_half = (kernel * assignment_weight[:, None] * packed[1][None, :]).astype(
            jnp.bfloat16
        )
        return (
            total + jnp.dot(transport_plan_half, packed[2], preferred_element_type=jnp.float32),
            None,
        )

    soft_half = lax.scan(
        soft_step, jnp.zeros((rows_here, feature_dim), jnp.float32), (blocks, scales, fresh_blocks)
    )[0]
    soft = lax.psum(soft_half, "cent")
    return (new_own, unit_tok - soft)


def solution(mesh):
    in_specs = (P("dp", None), P(("dp", "cent"), None))
    out_specs = (P(("dp", "cent"), None), P("dp", None))
    return jax.shard_map(shards, mesh=mesh, in_specs=in_specs, out_specs=out_specs, check_vma=False)
```

profile of v0, /device:TPU:1, one launch (start us, length us, event | category | flops | bytes accessed | tf_op | source)
XLA Modules:
  0.0 2422.9 jit_solution(2898249756367351308)
XLA Ops:
  11.5 130.1 %all-gather.6.cloned.1.call-done = bf16[16384,128]{1,0:T(8,128)(2,1)} async-done(((bf16[64,128]{1,0:T(8,128)(2,1)}), bf16[16384,128]{1,0:T(8,128)(2,1)}) %all-gather.6.cloned.1.call-update) | async-done | bytes 4194320 | tf_op jit(solution)/shard_map/all_gather | solution.py:28
  141.6 13.4 while.91
  155.1 6.3 psum.49
  161.3 14.4 while.88
  176.4 218.9 %all-reduce.5.cloned.1.call-done = f32[16384]{0:T(1024)} async-done(((f32[16384]{0:T(1024)}), f32[16384]{0:T(1024)}) %all-reduce.5.cloned.1.call-update) | async-done | bytes 65552 | tf_op jit(solution)/shard_map/psum | solution.py:50
  396.2 13.7 while.92
  409.9 7.2 psum.51
  417.1 14.4 while.89
  434.8 214.8 %all-reduce.7.cloned.1.call-done = f32[16384]{0:T(1024)} async-done(((f32[16384]{0:T(1024)}), f32[16384]{0:T(1024)}) %all-reduce.7.cloned.1.call-update) | async-done | bytes 65552 | tf_op jit(solution)/shard_map/psum | solution.py:50
  650.4 13.7 while.93
  664.1 7.2 psum.53
  671.6 1146.0 %all-reduce = bf16[30720]{0:T(1024)(128)(2,1)S(1)} all-reduce(bf16[30720]{0:T(1024)(128)(2,1)S(1)} %dynamic-update-slice), channel_id=1, replica_groups=mesh['dp'=256,'cent'=2] {'dp'}, use_global_device_ids=true, to_apply=%add | all-reduce | flops 30720 | bytes 122880
  1817.6 14.4 while.90
  1832.7 9.6 multiply_reduce_fusion.1
  1843.0 421.1 %all-reduce.9.cloned.1.call-done = f32[16384]{0:T(1024)} async-done(((f32[16384]{0:T(1024)}), f32[16384]{0:T(1024)}) %all-reduce.9.cloned.1.call-update) | async-done | bytes 65552 | tf_op jit(solution)/shard_map/psum | solution.py:50
  2265.0 126.2 %all-gather.8.cloned.1.call-done = bf16[16384,128]{1,0:T(8,128)(2,1)} async-done(((bf16[64,128]{1,0:T(8,128)(2,1)}), bf16[16384,128]{1,0:T(8,128)(2,1)}) %all-gather.8.cloned.1.call-update) | async-done | bytes 4194320 | tf_op jit(solution)/shard_map/all_gather | solution.py:63
  2391.2 16.6 while.94
  2391.2 2.0 fusion.144
  2393.3 2.0 fusion.144
  2395.4 2.0 fusion.144
  2397.4 2.0 fusion.144
  2399.5 2.0 fusion.144
  2401.6 2.0 fusion.144
  2407.8 7.5 psum.55
  (175 shorter events, 99.2 us)
Async XLA Ops:
  7.2 134.5 %all-gather.6.cloned.1.call-start = ((), (), s32[]{:S(2)}) async-start(), calls=%async_computation.1 | async-start | bytes 4210688 | tf_op jit(solution)/shard_map/all_gather | solution.py:28
  9.6 385.8 %all-reduce.5.cloned.1.call-start = ((), (), s32[]{:S(2)}) async-start(), calls=%async_computation.2 | async-start | bytes 131072 | tf_op jit(solution)/shard_map/psum | solution.py:50
  176.4 473.2 %all-reduce.7.cloned.1.call-start = ((), (), s32[]{:S(2)}) async-start(), calls=%async_computation.3 | async-start | bytes 131072 | tf_op jit(solution)/shard_map/psum | solution.py:50
  431.5 0.7 copy-start.1
  432.2 1400.5 %all-gather.4.cloned.1.call-start = ((), (), s32[]{:S(2)}) async-start(), calls=%async_computation | async-start | bytes 7895040 | tf_op jit(solution)/shard_map/all_gather | solution.py:54
  432.7 1831.4 %all-reduce.9.cloned.1.call-start = ((), (), s32[]{:S(2)}) async-start(), calls=%async_computation.4 | async-start | bytes 131072 | tf_op jit(solution)/shard_map/psum | solution.py:50
  1817.6 15.1 copy-start.3
  1832.6 558.6 %copy-start.2 = (bf16[120,128]{1,0:T(8,128)(2,1)S(1)}, bf16[120,128]{1,0:T(8,128)(2,1)}, u32[]{:S(2)}) copy-start(bf16[120,128]{1,0:T(8,128)(2,1)} %get-tuple-element.1021) | copy-start | bytes 92164
  1832.6 558.6 %all-gather.8.cloned.1.call-start = ((), (), s32[]{:S(2)}) async-start(), calls=%async_computation.5 | async-start | bytes 4210688 | tf_op jit(solution)/shard_map/all_gather | solution.py:63
  2391.2 24.1 copy-start
Sparse Core Ops, SparseCore 0:
  12.9 128.6 all-gather.5
  176.5 218.8 all-reduce.4
  432.3 217.2 all-reduce.6
  654.4 129.2 all-gather.3
  1832.7 431.3 all-reduce.8
  2269.1 122.0 all-gather.7
where the time goes:
time: 2430 us; the launch traced here: 2420 us
  blocking collectives  1170 us (48%)
  waiting for transfers between devices  1110 us (46%)
  matrix products  103 us (4%)
    unnamed x1, blocking collectives  1150 us
    psum x3, waiting for transfers between devices, shards(): col_total = lax.psum(col_flat, 'dp')  855 us
    all_gather x1, waiting for transfers between devices, shards(): columns = lax.all_gather(own_rows, 'dp', axis=0, tiled=True)  130 us
    all_gather x1, waiting for transfers between devices, shards(): lax.all_gather(new_own.astype(jnp.bfloat16), 'dp', axis=0, tiled=True)  126 us
    dot_general x48, matrix products, exponent_block(): lax.dot_general(token_half_rows, block, (((1,), (1,)), ((), ())), preferr...  77.1 us
  transfers between devices with their start and end apart: 6, of which 5 were waited for; matrix products, arithmetic and copies ran while one was open for 2% of the time, Pallas kernels for 0%

commit v1 on v0

--- a/solution.py
+++ b/solution.py
@@ -47,7 +47,8 @@
             return jnp.sum(kernel * assignment_weight[:, None], axis=0)
 
         col_flat = lax.map(col_only, blocks).reshape(col_count)
-        col_total = lax.psum(col_flat, "dp")
+        parts = lax.all_gather(col_flat, "dp")
+        col_total = jnp.sum(parts, axis=0)
         scales = (col_mass / col_total).reshape(block_count, KB)
     weights_bf = assignment_weight.astype(jnp.bfloat16)
     pieces = (

time: 2430 us -> 2100 us (0.86)
  waiting for transfers between devices: 1110 us -> 759 us
  other arithmetic: 8.49 us -> 42.3 us
    psum x3 -> x0, waiting for transfers between devices: 855 us -> none  [shards(): col_total = lax.psum(col_flat, 'dp')]
    all_gather x0 -> x3, waiting for transfers between devices: none -> 310 us  [shards(): parts = lax.all_gather(col_flat, 'dp')]
    all_gather x1, waiting for transfers between devices: 126 us -> 318 us  [shards(): lax.all_gather(new_own.astype(jnp.bfloat16), 'dp', axis=0, tiled=True)]
    reduce_sum x0 -> x3, other arithmetic: none -> 36.3 us  [shards(): col_total = jnp.sum(parts, axis=0)]
  transfers between devices with their start and end apart: 6 -> 6, of which waited for: 5 -> 4; matrix products, arithmetic and copies ran while one was open for 2% -> 3% of each run, Pallas kernels for 0% -> 0%
where the time goes in v1:
time: 2100 us
  blocking collectives  1170 us (56%)
  waiting for transfers between devices  759 us (36%)
  matrix products  102 us (5%)
  other arithmetic  42.3 us (2%)
    unnamed x1, blocking collectives  1150 us
    all_gather x1, waiting for transfers between devices, shards(): lax.all_gather(new_own.astype(jnp.bfloat16), 'dp', axis=0, tiled=True)  318 us
    all_gather x3, waiting for transfers between devices, shards(): parts = lax.all_gather(col_flat, 'dp')  310 us
    all_gather x1, waiting for transfers between devices, shards(): columns = lax.all_gather(own_rows, 'dp', axis=0, tiled=True)  130 us
    dot_general x48, matrix products, exponent_block(): lax.dot_general(token_half_rows, block, (((1,), (1,)), ((), ())), preferr...  77.2 us
  transfers between devices with their start and end apart: 6, of which 4 were waited for; matrix products, arithmetic and copies ran while one was open for 3% of the time, Pallas kernels for 0%

profile of v1, /device:TPU:1, one launch (start us, length us, event | category | flops | bytes accessed | tf_op | source)
XLA Modules:
  0.0 2097.4 jit_solution(9791629101928616582)
XLA Ops:
  11.5 130.1 %all-gather.12.cloned.1.call-done = bf16[16384,128]{1,0:T(8,128)(2,1)} async-done(((bf16[64,128]{1,0:T(8,128)(2,1)}), bf16[16384,128]{1,0:T(8,128)(2,1)}) %all-gather.12.cloned.1.call-update) | async-done | bytes 4194320 | tf_op jit(solution)/shard_map/all_gather | solution.py:28
  141.6 13.4 while.91
  155.1 6.3 psum.28
  161.3 14.4 while.88
  176.5 154.9 %all-gather.16.cloned.1.call-done = f32[256,1,16384]{2,1,0:T(1,128)} async-done(((f32[1,1,16384]{2,1,0:T(1,128)}), f32[256,1,16384]{2,1,0:T(1,128)}) %all-gather.16.cloned.1.call-update) | async-done | bytes 16777232 | tf_op jit(solution)/shard_map/all_gather | solution.py:50
  331.4 12.1 reduce_sum.128
  343.6 13.7 while.92
  357.3 3.3 psum.29
  360.6 14.4 while.89
  376.4 154.7 %all-gather.18.cloned.1.call-done = f32[256,1,16384]{2,1,0:T(1,128)} async-done(((f32[1,1,16384]{2,1,0:T(1,128)}), f32[256,1,16384]{2,1,0:T(1,128)}) %all-gather.18.cloned.1.call-update) | async-done | bytes 16777232 | tf_op jit(solution)/shard_map/all_gather | solution.py:50
  531.1 12.1 reduce_sum.129
  543.3 13.7 while.93
  557.0 3.3 psum.30
  560.4 14.4 while.90
  577.7 1148.6 %all-reduce = bf16[30720]{0:T(1024)(128)(2,1)S(1)} all-reduce(bf16[30720]{0:T(1024)(128)(2,1)S(1)} %dynamic-update-slice), channel_id=1, replica_groups=mesh['dp'=256,'cent'=2] {'dp'}, use_global_device_ids=true, to_apply=%add | all-reduce | flops 30720 | bytes 122880
  1726.3 9.6 multiply_reduce_fusion.1
  1736.7 12.1 reduce_sum.131
  1748.8 318.3 %all-gather.14.cloned.1.call-done = bf16[16384,128]{1,0:T(8,128)(2,1)} async-done(((bf16[64,128]{1,0:T(8,128)(2,1)}), bf16[16384,128]{1,0:T(8,128)(2,1)}) %all-gather.14.cloned.1.call-update) | async-done | bytes 4194320 | tf_op jit(solution)/shard_map/all_gather | solution.py:64
  2067.1 15.2 while.94
  2067.1 1.9 fusion.144
  2072.8 1.9 fusion.144
  2076.6 1.9 fusion.144
  2080.4 1.9 fusion.144
  2082.3 7.5 psum.31
  (178 shorter events, 100.3 us)
Async XLA Ops:
  7.2 134.5 %all-gather.12.cloned.1.call-start = ((), (), s32[]{:S(2)}) async-start(), calls=%async_computation.1 | async-start | bytes 4210688 | tf_op jit(solution)/shard_map/all_gather | solution.py:28
  9.6 321.9 %all-gather.16.cloned.1.call-start = ((), (), s32[]{:S(2)}) async-start(), calls=%async_computation.3 | async-start | bytes 16842752 | tf_op jit(solution)/shard_map/all_gather | solution.py:50
  176.4 354.7 %all-gather.18.cloned.1.call-start = ((), (), s32[]{:S(2)}) async-start(), calls=%async_computation.4 | async-start | bytes 16842752 | tf_op jit(solution)/shard_map/all_gather | solution.py:50
  375.0 0.8 copy-start.1
  375.7 1350.6 %all-gather.10.cloned.1.call-start = ((), (), s32[]{:S(2)}) async-start(), calls=%async_computation | async-start | bytes 7895040 | tf_op jit(solution)/shard_map/all_gather | solution.py:55
  376.3 1360.4 %all-gather.20.cloned.1.call-start = ((), (), s32[]{:S(2)}) async-start(), calls=%async_computation.5 | async-start | bytes 16842752 | tf_op jit(solution)/shard_map/all_gather | solution.py:50
  376.4 166.9 %copy-start.2 = (bf16[120,128]{1,0:T(8,128)(2,1)S(1)}, bf16[120,128]{1,0:T(8,128)(2,1)}, u32[]{:S(2)}) copy-start(bf16[120,128]{1,0:T(8,128)(2,1)} %copy-done.1) | copy-start | bytes 92164
  560.4 1166.0 %copy-start.3 = (bf16[64,128]{1,0:T(8,128)(2,1)S(1)}, bf16[64,128]{1,0:T(8,128)(2,1)}, u32[]{:S(2)}) copy-start(bf16[64,128]{1,0:T(8,128)(2,1)} %multiply_convert_fusion.1) | copy-start | bytes 49156
  575.5 1491.6 %all-gather.14.cloned.1.call-start = ((), (), s32[]{:S(2)}) async-start(), calls=%async_computation.2 | async-start | bytes 4210688 | tf_op jit(solution)/shard_map/all_gather | solution.py:64
  2067.1 22.7 %copy-start = (f32[120,128]{1,0:T(8,128)S(1)}, f32[120,128]{1,0:T(8,128)}, u32[]{:S(2)}) copy-start(f32[120,128]{1,0:T(8,128)} %param.16) | copy-start | bytes 184324
Sparse Core Ops, SparseCore 0:
  12.9 128.6 all-gather.11
  176.6 154.8 all-gather.15
  375.9 155.2 all-gather.17
  536.0 127.7 all-gather.9
  668.1 157.4 all-gather.19
  1736.8 330.2 all-gather.13
